TPU v7x, 32 devices: a whole 2x2x4 slice. The times are simulated.
32 devices in a mesh: section: 1, seq: 16 (over z, y, x), mp: 2 (over core).
Axes of the slice: x: 2, y: 2, z: 4, core: 2. Of those that a mesh axis runs over, the one named last changes fastest.
Arguments:
- hidden_in: bfloat16 [4096, 5376], P('seq'), may hold values from -30 to 30
- query_weight: bfloat16 [1, 5376, 2048], P('section', 'seq', 'mp'), may hold values from -0.078125 to 0.078125
- key_weight: bfloat16 [1, 5376, 1024], P('section', 'seq', 'mp'), may hold values from -0.078125 to 0.078125
- value_weight: bfloat16 [1, 5376, 1024], P('section', 'seq', 'mp'), may hold values from -0.078125 to 0.078125
- output_weight: bfloat16 [1, 2048, 5376], P('section', 'mp', 'seq'), may hold values from -0.5524272 to 0.5524272
- input_gain: bfloat16 [1, 5376], P('section'), may hold values from 0.099609375 to 1.8984375
- post_gain: bfloat16 [1, 5376], P('section', 'mp'), may hold values from 0.099609375 to 1.8984375
Outputs:
- hidden_out: bfloat16 [1, 4096, 5376], P('section', 'seq', 'mp')
All inputs are finite; a program needn't handle non-finite values.
Results may differ from a plain program's by a relative error of at most 0.013.
Values may be sent and summed in bfloat16 or wider, within the bound.
A program may use at most 128 MiB of HBM per device.

v0:
```python
import math
import jax
import jax.numpy as jnp
from jax import lax
from jax.sharding import PartitionSpec as P

HEADS = 16
KV_HEADS = 8
HEAD_DIM = 128
WINDOW = 1024
QSCALE = 168
NORM_EPS = 1e-06


def from_behind(block, axis, distance):
    devices = range(lax.axis_size(axis))
    route = [(i - distance, i) for i in devices if i - distance in devices]
    return lax.ppermute(block, axis, route)


def rope_tables(positions, head_size):
    half_dim = head_size // 2
    frequency = jnp.exp(
        -math.log(10000.0) * (2.0 * jnp.arange(half_dim, dtype=jnp.float32)) / head_size
    )
    angles = positions.astype(jnp.float32)[:, None] * frequency[None, :]
    return (jnp.cos(angles), jnp.sin(angles))


def norm_rotate(values, cosine, sine_table):
    scaled = values * lax.rsqrt(jnp.mean(values * values, axis=-1, keepdims=True) + NORM_EPS)
    half_dim = scaled.shape[-1] // 2
    leading = scaled[..., :half_dim]
    trailing = scaled[..., half_dim:]
    cosine = cosine[:, None, :]
    sine_table = sine_table[:, None, :]
    rotated = jnp.concatenate(
        [leading * cosine - trailing * sine_table, trailing * cosine + leading * sine_table],
        axis=-1,
    )
    return rotated.astype(jnp.bfloat16)


def body(hidden_in, query_weight, key_weight, value_weight, output_weight, input_gain, post_gain):
    row_count = hidden_in.shape[0]
    model_width = hidden_in.shape[1]
    half_width = post_gain.shape[1]
    core_index = lax.axis_index("mp")
    shard_index = lax.axis_index("seq")
    section_index = lax.axis_index("section")
    query_full, key_full, value_full = (
        lax.all_gather(query_weight[0], "seq", axis=0, tiled=True),
        lax.all_gather(key_weight[0], "seq", axis=0, tiled=True),
        lax.all_gather(value_weight[0], "seq", axis=0, tiled=True),
    )
    output_full = lax.all_gather(output_weight[0], "seq", axis=1, tiled=True)
    gain_first = input_gain[0].astype(jnp.float32)
    gain_second = post_gain[0].astype(jnp.float32)
    group_size = HEADS // KV_HEADS
    query_heads_local = query_full.shape[1] // HEAD_DIM
    local_heads = key_full.shape[1] // HEAD_DIM
    reach_shards = (WINDOW + row_count - 2) // row_count
    score_scale = 1.0 / math.sqrt(QSCALE)
    positions = shard_index * row_count + jnp.arange(row_count, dtype=jnp.int32)
    cosine, sine_table = rope_tables(positions, HEAD_DIM)
    key_positions = (
        shard_index * row_count
        - reach_shards * row_count
        + jnp.arange((reach_shards + 1) * row_count, dtype=jnp.int32)
    )
    distance = positions[:, None] - key_positions[None, :]
    visible = ((distance >= 0) & (distance < WINDOW) & (key_positions[None, :] >= 0)).astype(
        jnp.float32
    )

    def project_rows(full_rows):
        rows_float = full_rows.astype(jnp.float32)
        normed = (
            rows_float
            * lax.rsqrt(jnp.mean(rows_float * rows_float, axis=1, keepdims=True) + NORM_EPS)
            * gain_first
        ).astype(jnp.bfloat16)
        queries = jnp.dot(normed, query_full, preferred_element_type=jnp.float32)
        keys_raw = jnp.dot(normed, key_full, preferred_element_type=jnp.float32)
        values_raw = jnp.dot(normed, value_full, preferred_element_type=jnp.float32)
        query_heads = norm_rotate(
            queries.reshape(row_count, query_heads_local, HEAD_DIM), cosine, sine_table
        )
        key_heads = norm_rotate(
            keys_raw.reshape(row_count, local_heads, HEAD_DIM), cosine, sine_table
        )
        key_value = jnp.concatenate(
            [key_heads.reshape(row_count, -1), values_raw.astype(jnp.bfloat16)], axis=1
        )
        return (query_heads, key_value)

    def skip_rows(full_rows):
        return (
            jnp.zeros((row_count, query_heads_local, HEAD_DIM), jnp.bfloat16),
            jnp.zeros((row_count, 2 * local_heads * HEAD_DIM), jnp.bfloat16),
        )

    def attend_rows(query_heads, window_rows):
        window_count = window_rows.shape[0]
        key_block = window_rows[:, : local_heads * HEAD_DIM].reshape(
            window_count, local_heads, HEAD_DIM
        )
        value_block = window_rows[:, local_heads * HEAD_DIM :].reshape(
            window_count, local_heads, HEAD_DIM
        )
        grouped = query_heads.reshape(row_count, local_heads, group_size, HEAD_DIM)
        scores = (
            jnp.einsum("tkgd,skd->kgts", grouped, key_block, preferred_element_type=jnp.float32)
            * score_scale
        )
        weights_raw = jnp.exp(scores) * visible
        softmax_weights = (weights_raw / jnp.sum(weights_raw, axis=-1, keepdims=True)).astype(
            jnp.bfloat16
        )
        attended = jnp.einsum(
            "kgts,skd->tkgd", softmax_weights, value_block, preferred_element_type=jnp.float32
        )
        attended = attended.astype(jnp.bfloat16).reshape(row_count, -1)
        return jnp.dot(attended, output_full, preferred_element_type=jnp.float32)

    def skip_attend(query_heads, window_rows):
        return jnp.zeros((row_count, model_width), jnp.float32)

    def attend_layer(full_rows, residual_half, active):
        query_heads, key_value = lax.cond(active, project_rows, skip_rows, full_rows)
        pieces = [key_value]
        carried = key_value
        for offset in range(reach_shards):
            carried = from_behind(carried, "seq", 1)
            pieces = [carried] + pieces
        window_rows = jnp.concatenate(pieces, axis=0)
        partial_value = lax.cond(active, attend_rows, skip_attend, query_heads, window_rows)
        summed = lax.psum_scatter(
            partial_value.astype(jnp.bfloat16), "mp", scatter_dimension=1, tiled=True
        ).astype(jnp.float32)
        squares = lax.psum(jnp.sum(summed * summed, axis=1, keepdims=True), "mp")
        branch = summed * lax.rsqrt(squares / model_width + NORM_EPS) * gain_second
        return (residual_half.astype(jnp.float32) + branch).astype(jnp.bfloat16)

    own_half = lax.dynamic_slice_in_dim(hidden_in, core_index * half_width, half_width, 1)
    layer_one = attend_layer(hidden_in, own_half, section_index == 0)
    arrived = from_behind(layer_one, "section", 1)
    full_rows = lax.all_gather(arrived, "mp", axis=1, tiled=True)
    layer_two = attend_layer(full_rows, arrived, section_index == 1)
    result = jnp.where(section_index == 0, layer_one, layer_two)
    return result[None]


def solution(mesh):
    placed = (
        P("seq", None),
        P("section", "seq", "mp"),
        P("section", "seq", "mp"),
        P("section", "seq", "mp"),
        P("section", "mp", "seq"),
        P("section", None),
        P("section", "mp"),
    )
    return jax.shard_map(
        body, mesh=mesh, in_specs=placed, out_specs=P("section", "seq", "mp"), check_vma=False
    )
```

profile of v0, /device:TPU:0, one launch (start us, length us, event | category | flops | bytes accessed | tf_op | source)
XLA Modules:
  0.0 530.9 jit_solution(8867680530757714097)
XLA Ops:
  6.5 0.7 all-gather.9.cloned.1.call-update
  7.3 0.7 all-gather.11.cloned.1.call-update
  8.1 0.7 all-gather.13.cloned.1.call-update
  8.8 0.5 all-gather.15.cloned.1.call-update
  9.4 0.8 convert_reduce_fusion
  10.2 2.4 fusion.8
  12.6 0.5 multiply_cosine_fusion
  13.2 86.9 %all-gather.9.cloned.1.call-done = bf16[1,5376,512]{2,1,0:T(8,128)(2,1)} async-done(((bf16[1,336,512]{2,1,0:T(8,128)(2,1)}), bf16[1,5376,512]{2,1,0:T(8,128)(2,1)}) %all-gather.9.cloned.1.call-update) | async-done | bytes 5505040 | tf_op jit(solution)/shard_map/all_gather | solution.py:53
  100.1 5.0 fusion.13
  105.1 1.2 reshape.109
  106.3 0.3 multiply_reduce_fusion.1
  106.7 0.3 broadcast_multiply_fusion.1
  107.0 0.5 subtract_convert_fusion.1
  107.5 0.4 pad_maximum_fusion.1
  108.0 80.6 %all-gather.11.cloned.1.call-done = bf16[1,5376,512]{2,1,0:T(8,128)(2,1)} async-done(((bf16[1,336,512]{2,1,0:T(8,128)(2,1)}), bf16[1,5376,512]{2,1,0:T(8,128)(2,1)}) %all-gather.11.cloned.1.call-update) | async-done | bytes 5505040 | tf_op jit(solution)/shard_map/all_gather | solution.py:54
  188.6 4.2 fusion.30
  192.9 3.4 collective-permute-start
  196.3 15.0 %collective-permute-done = bf16[256,1024]{1,0:T(8,128)(2,1)S(1)} collective-permute-done((bf16[256,1024]{1,0:T(8,128)(2,1)S(1)}, bf16[256,1024]{1,0:T(8,128)(2,1)S(1)}, u32[]{:S(2)}, u32[]{:S(2)}) %collective-permute-start) | collective-permute-done | bytes 524320 | tf_op jit(solution)/shard_map/ppermute | solution.py:18
  211.3 4.4 collective-permute-start.1
  215.7 9.3 %collective-permute-done.1 = bf16[256,1024]{1,0:T(8,128)(2,1)S(1)} collective-permute-done((bf16[256,1024]{1,0:T(8,128)(2,1)S(1)}, bf16[256,1024]{1,0:T(8,128)(2,1)S(1)}, u32[]{:S(2)}, u32[]{:S(2)}) %collective-permute-start.1) | collective-permute-done | bytes 524320 | tf_op jit(solution)/shard_map/ppermute | solution.py:18
  225.0 5.2 collective-permute-start.2
  230.2 19.9 %collective-permute-done.2 = bf16[256,1024]{1,0:T(8,128)(2,1)} collective-permute-done((bf16[256,1024]{1,0:T(8,128)(2,1)S(1)}, bf16[256,1024]{1,0:T(8,128)(2,1)}, u32[]{:S(2)}, u32[]{:S(2)}) %collective-permute-start.2) | collective-permute-done | bytes 524320 | tf_op jit(solution)/shard_map/ppermute | solution.py:18
  250.1 4.7 collective-permute-start.3
  254.8 0.4 fusion.28
  255.2 13.6 %collective-permute-done.3 = bf16[256,1024]{1,0:T(8,128)(2,1)S(1)} collective-permute-done((bf16[256,1024]{1,0:T(8,128)(2,1)}, bf16[256,1024]{1,0:T(8,128)(2,1)S(1)}, u32[]{:S(2)}, u32[]{:S(2)}) %collective-permute-start.3) | collective-permute-done | bytes 524320 | tf_op jit(solution)/shard_map/ppermute | solution.py:18
  268.9 1.1 constant_dynamic-update-slice_fusion.3
  270.1 1.2 fusion.42
  271.3 3.6 reshape.110
  274.9 1.4 copy.44
  276.3 76.1 %all-gather.13.cloned.1.call-done = bf16[1,5376,1024]{2,1,0:T(8,128)(2,1)} async-done(((bf16[1,336,1024]{2,1,0:T(8,128)(2,1)}), bf16[1,5376,1024]{2,1,0:T(8,128)(2,1)}) %all-gather.13.cloned.1.call-update) | async-done | bytes 11010064 | tf_op jit(solution)/shard_map/all_gather | solution.py:52
  352.4 6.7 %fusion.21 = f32[32,8,8,128]{3,1,2,0:T(8,128)S(1)} fusion(bf16[1,5376,1024]{2,1,0:T(8,128)(2,1)} %all-gather.13.cloned.1.call-done, bf16[256,5376]{1,0:T(8,128)(2,1)} %param.7, f32[5376]{0:T(1024)S(1)} %copy-done.4, f32[256]{0:T(256)S(1)} %add_rsqrt_fusion.3), kind=kOutput, calls=%fused_computation.27 | convolution fusion | flops 2824077312 | bytes 14833664 | tf_op jit(solution)/shard_map/cond/branch_1_fun/dot_general | solution.py:83
  359.2 0.2 copy.48
  359.4 0.3 multiply_reduce_fusion
  359.8 0.2 copy.33
  359.9 0.3 broadcast_multiply_fusion
  360.3 0.5 subtract_convert_fusion
  360.9 0.6 copy-done.1
  361.6 2.6 fusion.4
  364.2 2.7 fusion.29
  366.9 126.6 %all-gather.15.cloned.1.call-done = bf16[1,1024,5376]{1,2,0:T(8,128)(2,1)} async-done(((bf16[1,1024,336]{1,2,0:T(8,128)(2,1)}), bf16[1,1024,5376]{1,2,0:T(8,128)(2,1)}) %all-gather.15.cloned.1.call-update) | async-done | bytes 11010064 | tf_op jit(solution)/shard_map/all_gather | solution.py:56
  493.5 11.6 %fusion.5 = bf16[256,5376]{1,0:T(8,128)(2,1)S(1)} fusion(bf16[256,1024]{0,1:T(8,128)(2,1)S(1)} %bitcast.66, bf16[1,1024,5376]{1,2,0:T(8,128)(2,1)} %all-gather.15.cloned.1.call-done), kind=kOutput, calls=%fused_computation.7 | convolution fusion | flops 2819948544 | bytes 14286848 | tf_op jit(solution)/shard_map/cond/branch_1_fun/dot_general | solution.py:124
  505.2 2.8 copy.45
  508.0 0.7 copy-done.5
  508.7 7.9 %reduce-scatter.4.cloned.1.call-done = bf16[2688,256]{1,0:T(8,128)(2,1)} async-done(((bf16[5376,256]{1,0:T(8,128)(2,1)}), bf16[2688,256]{1,0:T(8,128)(2,1)}) %reduce-scatter.4.cloned.1.call-update) | async-done | bytes 1376272
  516.7 1.8 copy.46
  518.5 0.4 fusion.16
  518.8 2.5 psum.6
  521.3 3.1 fusion.20
  (34 shorter events, 0.8 us)
Async XLA Ops:
  6.5 93.6 %copy-start = (bf16[256,5376]{1,0:T(8,128)(2,1)S(1)}, bf16[256,5376]{1,0:T(8,128)(2,1)}, u32[]{:S(2)}) copy-start(bf16[256,5376]{1,0:T(8,128)(2,1)} %param.7) | copy-start | bytes 8257540
  6.5 93.6 %all-gather.9.cloned.1.call-start = ((), (), s32[]{:S(2)}) async-start(), calls=%async_computation.1 | async-start | bytes 5849088 | tf_op jit(solution)/shard_map/all_gather | solution.py:53
  7.3 181.4 %all-gather.11.cloned.1.call-start = ((), (), s32[]{:S(2)}) async-start(), calls=%async_computation.2 | async-start | bytes 5849088 | tf_op jit(solution)/shard_map/all_gather | solution.py:54
  8.0 344.4 %all-gather.13.cloned.1.call-start = ((), (), s32[]{:S(2)}) async-start(), calls=%async_computation.3 | async-start | bytes 11698176 | tf_op jit(solution)/shard_map/all_gather | solution.py:52
  8.7 484.8 %all-gather.15.cloned.1.call-start = ((), (), s32[]{:S(2)}) async-start(), calls=%async_computation.4 | async-start | bytes 11698176 | tf_op jit(solution)/shard_map/all_gather | solution.py:56
  9.3 507.4 %reduce-scatter.4.cloned.1.call-start = ((), (), s32[]{:S(2)}) async-start(), calls=%async_computation.5 | async-start | bytes 4128768
  10.2 89.9 %copy-start.3 = (f32[5376]{0:T(1024)}, f32[5376]{0:T(1024)S(1)}, u32[]{:S(2)}) copy-start(f32[5376]{0:T(1024)S(1)} %convert_reduce_fusion) | copy-start | bytes 64516
  192.9 18.4 %collective-permute-start = (bf16[256,1024]{1,0:T(8,128)(2,1)S(1)}, bf16[256,1024]{1,0:T(8,128)(2,1)S(1)}, u32[]{:S(2)}, u32[]{:S(2)}) collective-permute-start(bf16[256,1024]{1,0:T(8,128)(2,1)S(1)} %pad_maximum_fusion), channel_id=1, source_target_pairs={{0,2},{2,4},{4,6},{6,8},{8,10},{10,12},{12,14},{14,16},{16,18},{18... | collective-permute-start | bytes 1572872 | tf_op jit(solution)/shard_map/ppermute | solution.py:18
  211.3 13.7 %collective-permute-start.1 = (bf16[256,1024]{1,0:T(8,128)(2,1)S(1)}, bf16[256,1024]{1,0:T(8,128)(2,1)S(1)}, u32[]{:S(2)}, u32[]{:S(2)}) collective-permute-start(bf16[256,1024]{1,0:T(8,128)(2,1)S(1)} %collective-permute-done), channel_id=1, source_target_pairs={{0,2},{2,4},{4,6},{6,8},{8,10},{10,12},{12,14},{14,16},{16,18},{18... | collective-permute-start | bytes 1572872 | tf_op jit(solution)/shard_map/ppermute | solution.py:18
  225.0 25.1 %collective-permute-start.2 = (bf16[256,1024]{1,0:T(8,128)(2,1)S(1)}, bf16[256,1024]{1,0:T(8,128)(2,1)}, u32[]{:S(2)}, u32[]{:S(2)}) collective-permute-start(bf16[256,1024]{1,0:T(8,128)(2,1)S(1)} %collective-permute-done.1), channel_id=1, source_target_pairs={{0,2},{2,4},{4,6},{6,8},{8,10},{10,12},{12,14},{14,16},{16,18},{18... | collective-permute-start | bytes 1572872 | tf_op jit(solution)/shard_map/ppermute | solution.py:18
  250.1 18.7 %collective-permute-start.3 = (bf16[256,1024]{1,0:T(8,128)(2,1)}, bf16[256,1024]{1,0:T(8,128)(2,1)S(1)}, u32[]{:S(2)}, u32[]{:S(2)}) collective-permute-start(bf16[256,1024]{1,0:T(8,128)(2,1)} %collective-permute-done.2), channel_id=1, source_target_pairs={{0,2},{2,4},{4,6},{6,8},{8,10},{10,12},{12,14},{14,16},{16,18},{18... | collective-permute-start | bytes 1572872 | tf_op jit(solution)/shard_map/ppermute | solution.py:18
  271.3 81.1 %copy-start.4 = (f32[5376]{0:T(1024)S(1)}, f32[5376]{0:T(1024)}, u32[]{:S(2)}) copy-start(f32[5376]{0:T(1024)} %copy-done.3) | copy-start | bytes 64516
  360.3 1.3 copy-start.1
  361.6 2.6 copy-start.2
  508.0 0.7 copy-start.5
Sparse Core Ops, SparseCore 0:
  10.2 89.9 all-gather.8
  102.9 85.6 all-gather.10
  191.4 160.9 all-gather.12
  355.1 138.3 all-gather.14
  508.2 8.4 reduce-scatter.3
where the time goes:
time: 532 us; the launch traced here: 531 us
  waiting for transfers between devices  439 us (83%)
  matrix products  32.9 us (6%)
  starting transfers between devices  17.8 us (3%)
  local copies, waits for them, and re-layouts  15.2 us (3%)
  between operations  13.4 us (3%)
  other arithmetic  10.6 us (2%)
    all_gather x1, waiting for transfers between devices, body(): output_full = lax.all_gather(output_weight[0], 'seq', axis=1, tiled=True)  127 us
    all_gather x1, waiting for transfers between devices, body(): lax.all_gather(key_weight[0], 'seq', axis=0, tiled=True)  86.9 us
    all_gather x1, waiting for transfers between devices, body(): lax.all_gather(value_weight[0], 'seq', axis=0, tiled=True)  80.6 us
    all_gather x1, waiting for transfers between devices, body(): lax.all_gather(query_weight[0], 'seq', axis=0, tiled=True)  76.1 us
    ppermute x4, waiting for transfers between devices, from_behind(): return lax.ppermute(block, axis, route)  57.8 us
    ppermute x4, starting transfers between devices, from_behind(): return lax.ppermute(block, axis, route)  17.7 us
    dot_general x1, matrix products, attend_rows(): return jnp.dot(attended, output_full, preferred_element_type=jnp.float32)  11.6 us
  transfers between devices with their start and end apart: 9, of which 9 were waited for; matrix products, arithmetic and copies ran while one was open for 7% of the time, Pallas kernels for 0%

commit v1 on v0

--- a/solution.py
+++ b/solution.py
@@ -10,6 +10,19 @@
 WINDOW = 1024
 QSCALE = 168
 NORM_EPS = 1e-06
+
+
+def ring_gather(shard, axis, dim):
+    peers, index, rows = (lax.axis_size(axis), lax.axis_index(axis), shard.shape[dim])
+    ahead = [(i, (i + 1) % peers) for i in range(peers)]
+    out = jnp.zeros((*shard.shape[:dim], peers * rows, *shard.shape[dim + 1 :]), shard.dtype)
+    held = shard
+    for hop in range(peers):
+        owner = (index - hop) % peers
+        out = lax.dynamic_update_slice_in_dim(out, held, owner * rows, axis=dim)
+        if hop < peers - 1:
+            held = lax.ppermute(held, axis, ahead)
+    return out
 
 
 def from_behind(block, axis, distance):
@@ -50,7 +63,7 @@
     section_index = lax.axis_index("section")
     query_full, key_full, value_full = (
         lax.all_gather(query_weight[0], "seq", axis=0, tiled=True),
-        lax.all_gather(key_weight[0], "seq", axis=0, tiled=True),
+        ring_gather(key_weight[0], "seq", 0),
         lax.all_gather(value_weight[0], "seq", axis=0, tiled=True),
     )
     output_full = lax.all_gather(output_weight[0], "seq", axis=1, tiled=True)

time: 532 us -> 514 us (0.966)
  waiting for transfers between devices: 439 us -> 413 us
  local copies, waits for them, and re-layouts: 15.2 us -> 24 us
    ppermute x0 -> x15, waiting for transfers between devices: none -> 262 us  [ring_gather(): held = lax.ppermute(held, axis, ahead)]
    all_gather x1 -> x0, waiting for transfers between devices: 86.9 us -> none  [body(): lax.all_gather(key_weight[0], 'seq', axis=0, tiled=True)]
    all_gather x1, waiting for transfers between devices: 80.6 us -> 0.02 us  [body(): lax.all_gather(value_weight[0], 'seq', axis=0, tiled=True)]
    all_gather x1, waiting for transfers between devices: 76.1 us -> 0.01 us  [body(): lax.all_gather(query_weight[0], 'seq', axis=0, tiled=True)]
    ppermute x4, waiting for transfers between devices: 57.8 us -> 33.5 us  [from_behind(): return lax.ppermute(block, axis, route)]
    all_gather x1, waiting for transfers between devices: 127 us -> 107 us  [body(): output_full = lax.all_gather(output_weight[0], 'seq', axis=1, tiled=True)]
    dynamic_update_slice x0 -> x16, local copies, waits for them, and re-layouts: none -> 7.3 us  [ring_gather(): out = lax.dynamic_update_slice_in_dim(out, held, owner * rows, axis=dim)]
    unnamed x6 -> x5, waiting for transfers between devices: 10.6 us -> 10.8 us
  transfers between devices with their start and end apart: 9 -> 23, of which waited for: 9 -> 21; matrix products, arithmetic and copies ran while one was open for 7% -> 8% of each run, Pallas kernels for 0% -> 0%
where the time goes in v1:
time: 514 us; the launch traced here: 513 us
  waiting for transfers between devices  413 us (80%)
  matrix products  30.9 us (6%)
  local copies, waits for them, and re-layouts  24 us (5%)
  starting transfers between devices  18.8 us (4%)
  between operations  13.7 us (3%)
  other arithmetic  9.79 us (2%)
    ppermute x15, waiting for transfers between devices, ring_gather(): held = lax.ppermute(held, axis, ahead)  262 us
    all_gather x1, waiting for transfers between devices, body(): output_full = lax.all_gather(output_weight[0], 'seq', axis=1, tiled=True)  107 us
    ppermute x4, waiting for transfers between devices, from_behind(): return lax.ppermute(block, axis, route)  33.5 us
    ppermute x4, starting transfers between devices, from_behind(): return lax.ppermute(block, axis, route)  15.6 us
    dot_general x1, matrix products, attend_rows(): return jnp.dot(attended, output_full, preferred_element_type=jnp.float32)  11.6 us
    unnamed x5, waiting for transfers between devices  10.8 us
  transfers between devices with their start and end apart: 23, of which 21 were waited for; matrix products, arithmetic and copies ran while one was open for 8% of the time, Pallas kernels for 0%

profile of v1, /device:TPU:0, one launch (start us, length us, event | category | flops | bytes accessed | tf_op | source)
XLA Modules:
  0.0 512.9 jit_solution(8479669559525064834)
XLA Ops:
  8.8 3.0 collective-permute-start
  11.8 12.3 %collective-permute-done = bf16[336,512]{1,0:T(8,128)(2,1)S(1)} collective-permute-done((bf16[336,512]{1,0:T(8,128)(2,1)}, bf16[336,512]{1,0:T(8,128)(2,1)S(1)}, u32[]{:S(2)}, u32[]{:S(2)}) %collective-permute-start) | collective-permute-done | bytes 344096 | tf_op jit(solution)/shard_map/ppermute | solution.py:24
  24.8 18.0 %collective-permute-done.1 = bf16[336,512]{1,0:T(8,128)(2,1)S(1)} collective-permute-done((bf16[336,512]{1,0:T(8,128)(2,1)S(1)}, bf16[336,512]{1,0:T(8,128)(2,1)S(1)}, u32[]{:S(2)}, u32[]{:S(2)}) %collective-permute-start.1) | collective-permute-done | bytes 344096 | tf_op jit(solution)/shard_map/ppermute | solution.py:24
  42.8 21.0 %collective-permute-done.2 = bf16[336,512]{1,0:T(8,128)(2,1)} collective-permute-done((bf16[336,512]{1,0:T(8,128)(2,1)S(1)}, bf16[336,512]{1,0:T(8,128)(2,1)}, u32[]{:S(2)}, u32[]{:S(2)}) %collective-permute-start.2) | collective-permute-done | bytes 344096 | tf_op jit(solution)/shard_map/ppermute | solution.py:24
  63.8 14.4 %collective-permute-done.3 = bf16[336,512]{1,0:T(8,128)(2,1)S(1)} collective-permute-done((bf16[336,512]{1,0:T(8,128)(2,1)}, bf16[336,512]{1,0:T(8,128)(2,1)S(1)}, u32[]{:S(2)}, u32[]{:S(2)}) %collective-permute-start.3) | collective-permute-done | bytes 344096 | tf_op jit(solution)/shard_map/ppermute | solution.py:24
  78.9 20.6 %collective-permute-done.4 = bf16[336,512]{1,0:T(8,128)(2,1)S(1)} collective-permute-done((bf16[336,512]{1,0:T(8,128)(2,1)S(1)}, bf16[336,512]{1,0:T(8,128)(2,1)S(1)}, u32[]{:S(2)}, u32[]{:S(2)}) %collective-permute-start.4) | collective-permute-done | bytes 344096 | tf_op jit(solution)/shard_map/ppermute | solution.py:24
  99.5 17.1 %collective-permute-done.5 = bf16[336,512]{1,0:T(8,128)(2,1)S(1)} collective-permute-done((bf16[336,512]{1,0:T(8,128)(2,1)S(1)}, bf16[336,512]{1,0:T(8,128)(2,1)S(1)}, u32[]{:S(2)}, u32[]{:S(2)}) %collective-permute-start.5) | collective-permute-done | bytes 344096 | tf_op jit(solution)/shard_map/ppermute | solution.py:24
  117.4 14.8 %collective-permute-done.6 = bf16[336,512]{1,0:T(8,128)(2,1)S(1)} collective-permute-done((bf16[336,512]{1,0:T(8,128)(2,1)S(1)}, bf16[336,512]{1,0:T(8,128)(2,1)S(1)}, u32[]{:S(2)}, u32[]{:S(2)}) %collective-permute-start.6) | collective-permute-done | bytes 344096 | tf_op jit(solution)/shard_map/ppermute | solution.py:24
  132.2 15.4 %collective-permute-done.7 = bf16[336,512]{1,0:T(8,128)(2,1)S(1)} collective-permute-done((bf16[336,512]{1,0:T(8,128)(2,1)S(1)}, bf16[336,512]{1,0:T(8,128)(2,1)S(1)}, u32[]{:S(2)}, u32[]{:S(2)}) %collective-permute-start.7) | collective-permute-done | bytes 344096 | tf_op jit(solution)/shard_map/ppermute | solution.py:24
  148.2 2.4 fusion.8
  150.6 16.4 %collective-permute-done.8 = bf16[336,512]{1,0:T(8,128)(2,1)} collective-permute-done((bf16[336,512]{1,0:T(8,128)(2,1)S(1)}, bf16[336,512]{1,0:T(8,128)(2,1)}, u32[]{:S(2)}, u32[]{:S(2)}) %collective-permute-start.8) | collective-permute-done | bytes 344096 | tf_op jit(solution)/shard_map/ppermute | solution.py:24
  167.4 20.1 %collective-permute-done.9 = bf16[336,512]{1,0:T(8,128)(2,1)} collective-permute-done((bf16[336,512]{1,0:T(8,128)(2,1)}, bf16[336,512]{1,0:T(8,128)(2,1)}, u32[]{:S(2)}, u32[]{:S(2)}) %collective-permute-start.9) | collective-permute-done | bytes 344096 | tf_op jit(solution)/shard_map/ppermute | solution.py:24
  187.8 21.1 %collective-permute-done.10 = bf16[336,512]{1,0:T(8,128)(2,1)S(1)} collective-permute-done((bf16[336,512]{1,0:T(8,128)(2,1)}, bf16[336,512]{1,0:T(8,128)(2,1)S(1)}, u32[]{:S(2)}, u32[]{:S(2)}) %collective-permute-start.10) | collective-permute-done | bytes 344096 | tf_op jit(solution)/shard_map/ppermute | solution.py:24
  208.8 1.0 constant_dynamic-update-slice_fusion.17
  209.8 1.0 constant_dynamic-update-slice_fusion.16
  210.8 1.0 constant_dynamic-update-slice_fusion.15
  211.9 13.8 %collective-permute-done.11 = bf16[336,512]{1,0:T(8,128)(2,1)S(1)} collective-permute-done((bf16[336,512]{1,0:T(8,128)(2,1)S(1)}, bf16[336,512]{1,0:T(8,128)(2,1)S(1)}, u32[]{:S(2)}, u32[]{:S(2)}) %collective-permute-start.11) | collective-permute-done | bytes 344096 | tf_op jit(solution)/shard_map/ppermute | solution.py:24
  225.6 1.0 constant_dynamic-update-slice_fusion.14
  226.7 1.0 constant_dynamic-update-slice_fusion.13
  227.7 19.6 %collective-permute-done.12 = bf16[336,512]{1,0:T(8,128)(2,1)S(1)} collective-permute-done((bf16[336,512]{1,0:T(8,128)(2,1)S(1)}, bf16[336,512]{1,0:T(8,128)(2,1)S(1)}, u32[]{:S(2)}, u32[]{:S(2)}) %collective-permute-start.12) | collective-permute-done | bytes 344096 | tf_op jit(solution)/shard_map/ppermute | solution.py:24
  248.3 1.0 constant_dynamic-update-slice_fusion.10
  249.4 19.3 %collective-permute-done.13 = bf16[336,512]{1,0:T(8,128)(2,1)S(1)} collective-permute-done((bf16[336,512]{1,0:T(8,128)(2,1)S(1)}, bf16[336,512]{1,0:T(8,128)(2,1)S(1)}, u32[]{:S(2)}, u32[]{:S(2)}) %collective-permute-start.13) | collective-permute-done | bytes 344096 | tf_op jit(solution)/shard_map/ppermute | solution.py:24
  268.8 18.0 %collective-permute-done.14 = bf16[336,512]{1,0:T(8,128)(2,1)S(1)} collective-permute-done((bf16[336,512]{1,0:T(8,128)(2,1)S(1)}, bf16[336,512]{1,0:T(8,128)(2,1)S(1)}, u32[]{:S(2)}, u32[]{:S(2)}) %collective-permute-start.14) | collective-permute-done | bytes 344096 | tf_op jit(solution)/shard_map/ppermute | solution.py:24
  286.9 2.5 fusion.39
  289.4 1.2 reshape.109
  292.3 4.2 fusion.28
  296.6 1.3 collective-permute-start.15
  297.9 9.5 %collective-permute-done.15 = bf16[256,1024]{1,0:T(8,128)(2,1)S(1)} collective-permute-done((bf16[256,1024]{1,0:T(8,128)(2,1)S(1)}, bf16[256,1024]{1,0:T(8,128)(2,1)S(1)}, u32[]{:S(2)}, u32[]{:S(2)}) %collective-permute-start.15) | collective-permute-done | bytes 524320 | tf_op jit(solution)/shard_map/ppermute | solution.py:31
  307.4 4.4 collective-permute-start.16
  311.8 10.3 %collective-permute-done.16 = bf16[256,1024]{1,0:T(8,128)(2,1)S(1)} collective-permute-done((bf16[256,1024]{1,0:T(8,128)(2,1)S(1)}, bf16[256,1024]{1,0:T(8,128)(2,1)S(1)}, u32[]{:S(2)}, u32[]{:S(2)}) %collective-permute-start.16) | collective-permute-done | bytes 524320 | tf_op jit(solution)/shard_map/ppermute | solution.py:31
  322.1 5.2 %collective-permute-start.17 = (bf16[256,1024]{1,0:T(8,128)(2,1)S(1)}, bf16[256,1024]{1,0:T(8,128)(2,1)}, u32[]{:S(2)}, u32[]{:S(2)}) collective-permute-start(bf16[256,1024]{1,0:T(8,128)(2,1)S(1)} %collective-permute-done.16), channel_id=1, source_target_pairs={{0,2},{2,4},{4,6},{6,8},{8,10},{10,12},{12,14},{14,16},{16,18},{18... | collective-permute-start | bytes 1572872 | tf_op jit(solution)/shard_map/ppermute | solution.py:31
  327.3 7.3 %collective-permute-done.17 = bf16[256,1024]{1,0:T(8,128)(2,1)} collective-permute-done((bf16[256,1024]{1,0:T(8,128)(2,1)S(1)}, bf16[256,1024]{1,0:T(8,128)(2,1)}, u32[]{:S(2)}, u32[]{:S(2)}) %collective-permute-start.17) | collective-permute-done | bytes 524320 | tf_op jit(solution)/shard_map/ppermute | solution.py:31
  334.6 4.7 collective-permute-start.18
  339.8 6.4 %collective-permute-done.18 = bf16[256,1024]{1,0:T(8,128)(2,1)S(1)} collective-permute-done((bf16[256,1024]{1,0:T(8,128)(2,1)}, bf16[256,1024]{1,0:T(8,128)(2,1)S(1)}, u32[]{:S(2)}, u32[]{:S(2)}) %collective-permute-start.18) | collective-permute-done | bytes 524320 | tf_op jit(solution)/shard_map/ppermute | solution.py:31
  346.2 1.1 constant_dynamic-update-slice_fusion.3
  347.4 1.2 fusion.41
  348.6 3.6 reshape.110
  352.2 1.4 copy.44
  353.6 7.3 %fusion.19 = f32[32,8,8,128]{3,1,2,0:T(8,128)S(1)} fusion(bf16[1,5376,1024]{2,1,0:T(8,128)(2,1)} %all-gather.9.cloned.1.call-done, bf16[256,5376]{1,0:T(8,128)(2,1)} %param.7, f32[5376]{0:T(1024)S(1)} %copy-done.15, f32[256]{0:T(256)S(1)} %add_rsqrt_fusion.3), kind=kOutput, calls=%fused_computation.25 | convolution fusion | flops 2824077312 | bytes 14833664 | tf_op jit(solution)/shard_map/cond/branch_1_fun/dot_general | solution.py:96
  363.0 2.6 fusion.4
  365.6 2.7 fusion.27
  368.3 107.1 %all-gather.11.cloned.1.call-done = bf16[1,1024,5376]{1,2,0:T(8,128)(2,1)} async-done(((bf16[1,1024,336]{1,2,0:T(8,128)(2,1)}), bf16[1,1024,5376]{1,2,0:T(8,128)(2,1)}) %all-gather.11.cloned.1.call-update) | async-done | bytes 11010064 | tf_op jit(solution)/shard_map/all_gather | solution.py:69
  475.5 11.6 %fusion.5 = bf16[256,5376]{1,0:T(8,128)(2,1)S(1)} fusion(bf16[256,1024]{0,1:T(8,128)(2,1)S(1)} %bitcast.67, bf16[1,1024,5376]{1,2,0:T(8,128)(2,1)} %all-gather.11.cloned.1.call-done), kind=kOutput, calls=%fused_computation.7 | convolution fusion | flops 2819948544 | bytes 14286848 | tf_op jit(solution)/shard_map/cond/branch_1_fun/dot_general | solution.py:137
  487.1 2.8 copy.45
  490.0 8.7 %reduce-scatter.4.cloned.1.call-done = bf16[2688,256]{1,0:T(8,128)(2,1)} async-done(((bf16[5376,256]{1,0:T(8,128)(2,1)}), bf16[2688,256]{1,0:T(8,128)(2,1)}) %reduce-scatter.4.cloned.1.call-update) | async-done | bytes 1376272
  498.7 1.8 copy.46
  500.8 2.5 psum.6
  503.3 3.1 fusion.18
  (102 shorter events, 11.5 us)
Async XLA Ops:
  6.5 160.8 %copy-start.3 = (bf16[1,336,512]{2,1,0:T(8,128)(2,1)S(1)}, bf16[1,336,512]{2,1,0:T(8,128)(2,1)}, u32[]{:S(2)}) copy-start(bf16[1,336,512]{2,1,0:T(8,128)(2,1)} %param.9) | copy-start | bytes 1032196
  6.5 285.8 %all-gather.7.cloned.1.call-start = ((), (), s32[]{:S(2)}) async-start(), calls=%async_computation.1 | async-start | bytes 5849088 | tf_op jit(solution)/shard_map/all_gather | solution.py:67
  7.3 180.3 %copy-start.16 = (bf16[1,5376]{1,0:T(2,128)(2,1)S(1)}, bf16[1,5376]{1,0:T(2,128)(2,1)}, u32[]{:S(2)}) copy-start(bf16[1,5376]{1,0:T(2,128)(2,1)} %param.12) | copy-start | bytes 32260
  7.3 346.3 %all-gather.9.cloned.1.call-start = ((), (), s32[]{:S(2)}) async-start(), calls=%async_computation.2 | async-start | bytes 11698176 | tf_op jit(solution)/shard_map/all_gather | solution.py:65
  8.0 467.4 %all-gather.11.cloned.1.call-start = ((), (), s32[]{:S(2)}) async-start(), calls=%async_computation.3 | async-start | bytes 11698176 | tf_op jit(solution)/shard_map/all_gather | solution.py:69
  8.8 489.9 %reduce-scatter.4.cloned.1.call-start = ((), (), s32[]{:S(2)}) async-start(), calls=%async_computation.4 | async-start | bytes 4128768
  8.8 15.3 %collective-permute-start = (bf16[336,512]{1,0:T(8,128)(2,1)}, bf16[336,512]{1,0:T(8,128)(2,1)S(1)}, u32[]{:S(2)}, u32[]{:S(2)}) collective-permute-start(bf16[336,512]{1,0:T(8,128)(2,1)} %bitcast.64), channel_id=1, source_target_pairs={{0,2},{2,4},{4,6},{6,8},{8,10},{10,12},{12,14},{14,16},{16,18},{18... | collective-permute-start | bytes 1032200 | tf_op jit(solution)/shard_map/ppermute | solution.py:24
  24.1 0.7 copy-start.4
  24.8 18.0 %collective-permute-start.1 = (bf16[336,512]{1,0:T(8,128)(2,1)S(1)}, bf16[336,512]{1,0:T(8,128)(2,1)S(1)}, u32[]{:S(2)}, u32[]{:S(2)}) collective-permute-start(bf16[336,512]{1,0:T(8,128)(2,1)S(1)} %collective-permute-done), channel_id=1, source_target_pairs={{0,2},{2,4},{4,6},{6,8},{8,10},{10,12},{12,14},{14,16},{16,18},{18... | collective-permute-start | bytes 1032200 | tf_op jit(solution)/shard_map/ppermute | solution.py:24
  42.8 89.4 %copy-start.8 = (bf16[336,512]{1,0:T(8,128)(2,1)}, bf16[336,512]{1,0:T(8,128)(2,1)S(1)}, u32[]{:S(2)}) copy-start(bf16[336,512]{1,0:T(8,128)(2,1)S(1)} %collective-permute-done.1) | copy-start | bytes 1032196
  42.8 21.0 %collective-permute-start.2 = (bf16[336,512]{1,0:T(8,128)(2,1)S(1)}, bf16[336,512]{1,0:T(8,128)(2,1)}, u32[]{:S(2)}, u32[]{:S(2)}) collective-permute-start(bf16[336,512]{1,0:T(8,128)(2,1)S(1)} %collective-permute-done.1), channel_id=1, source_target_pairs={{0,2},{2,4},{4,6},{6,8},{8,10},{10,12},{12,14},{14,16},{16,18},{18... | collective-permute-start | bytes 1032200 | tf_op jit(solution)/shard_map/ppermute | solution.py:24
  63.8 14.4 %collective-permute-start.3 = (bf16[336,512]{1,0:T(8,128)(2,1)}, bf16[336,512]{1,0:T(8,128)(2,1)S(1)}, u32[]{:S(2)}, u32[]{:S(2)}) collective-permute-start(bf16[336,512]{1,0:T(8,128)(2,1)} %collective-permute-done.2), channel_id=1, source_target_pairs={{0,2},{2,4},{4,6},{6,8},{8,10},{10,12},{12,14},{14,16},{16,18},{18... | collective-permute-start | bytes 1032200 | tf_op jit(solution)/shard_map/ppermute | solution.py:24
  78.2 0.7 copy-start.7
  78.2 21.3 %collective-permute-start.4 = (bf16[336,512]{1,0:T(8,128)(2,1)S(1)}, bf16[336,512]{1,0:T(8,128)(2,1)S(1)}, u32[]{:S(2)}, u32[]{:S(2)}) collective-permute-start(bf16[336,512]{1,0:T(8,128)(2,1)S(1)} %collective-permute-done.3), channel_id=1, source_target_pairs={{0,2},{2,4},{4,6},{6,8},{8,10},{10,12},{12,14},{14,16},{16,18},{18... | collective-permute-start | bytes 1032200 | tf_op jit(solution)/shard_map/ppermute | solution.py:24
  99.5 32.6 %copy-start.11 = (bf16[336,512]{1,0:T(8,128)(2,1)}, bf16[336,512]{1,0:T(8,128)(2,1)S(1)}, u32[]{:S(2)}) copy-start(bf16[336,512]{1,0:T(8,128)(2,1)S(1)} %collective-permute-done.4) | copy-start | bytes 1032196
  99.5 17.1 %collective-permute-start.5 = (bf16[336,512]{1,0:T(8,128)(2,1)S(1)}, bf16[336,512]{1,0:T(8,128)(2,1)S(1)}, u32[]{:S(2)}, u32[]{:S(2)}) collective-permute-start(bf16[336,512]{1,0:T(8,128)(2,1)S(1)} %collective-permute-done.4), channel_id=1, source_target_pairs={{0,2},{2,4},{4,6},{6,8},{8,10},{10,12},{12,14},{14,16},{16,18},{18... | collective-permute-start | bytes 1032200 | tf_op jit(solution)/shard_map/ppermute | solution.py:24
  116.6 0.7 copy-start.6
  117.4 14.8 %collective-permute-start.6 = (bf16[336,512]{1,0:T(8,128)(2,1)S(1)}, bf16[336,512]{1,0:T(8,128)(2,1)S(1)}, u32[]{:S(2)}, u32[]{:S(2)}) collective-permute-start(bf16[336,512]{1,0:T(8,128)(2,1)S(1)} %collective-permute-done.5), channel_id=1, source_target_pairs={{0,2},{2,4},{4,6},{6,8},{8,10},{10,12},{12,14},{14,16},{16,18},{18... | collective-permute-start | bytes 1032200 | tf_op jit(solution)/shard_map/ppermute | solution.py:24
  132.1 34.8 %copy-start.10 = (bf16[336,512]{1,0:T(8,128)(2,1)}, bf16[336,512]{1,0:T(8,128)(2,1)S(1)}, u32[]{:S(2)}) copy-start(bf16[336,512]{1,0:T(8,128)(2,1)S(1)} %collective-permute-done.6) | copy-start | bytes 1032196
  132.2 15.5 %collective-permute-start.7 = (bf16[336,512]{1,0:T(8,128)(2,1)S(1)}, bf16[336,512]{1,0:T(8,128)(2,1)S(1)}, u32[]{:S(2)}, u32[]{:S(2)}) collective-permute-start(bf16[336,512]{1,0:T(8,128)(2,1)S(1)} %collective-permute-done.6), channel_id=1, source_target_pairs={{0,2},{2,4},{4,6},{6,8},{8,10},{10,12},{12,14},{14,16},{16,18},{18... | collective-permute-start | bytes 1032200 | tf_op jit(solution)/shard_map/ppermute | solution.py:24
  147.6 19.3 %copy-start.12 = (bf16[336,512]{1,0:T(8,128)(2,1)}, bf16[336,512]{1,0:T(8,128)(2,1)S(1)}, u32[]{:S(2)}) copy-start(bf16[336,512]{1,0:T(8,128)(2,1)S(1)} %collective-permute-done.7) | copy-start | bytes 1032196
  147.6 19.3 %collective-permute-start.8 = (bf16[336,512]{1,0:T(8,128)(2,1)S(1)}, bf16[336,512]{1,0:T(8,128)(2,1)}, u32[]{:S(2)}, u32[]{:S(2)}) collective-permute-start(bf16[336,512]{1,0:T(8,128)(2,1)S(1)} %collective-permute-done.7), channel_id=1, source_target_pairs={{0,2},{2,4},{4,6},{6,8},{8,10},{10,12},{12,14},{14,16},{16,18},{18... | collective-permute-start | bytes 1032200 | tf_op jit(solution)/shard_map/ppermute | solution.py:24
  167.0 20.6 %collective-permute-start.9 = (bf16[336,512]{1,0:T(8,128)(2,1)}, bf16[336,512]{1,0:T(8,128)(2,1)}, u32[]{:S(2)}, u32[]{:S(2)}) collective-permute-start(bf16[336,512]{1,0:T(8,128)(2,1)} %collective-permute-done.8), channel_id=1, source_target_pairs={{0,2},{2,4},{4,6},{6,8},{8,10},{10,12},{12,14},{14,16},{16,18},{18... | collective-permute-start | bytes 1032200 | tf_op jit(solution)/shard_map/ppermute | solution.py:24
  167.0 20.7 %copy-start.5 = (bf16[336,512]{1,0:T(8,128)(2,1)S(1)}, bf16[336,512]{1,0:T(8,128)(2,1)}, u32[]{:S(2)}) copy-start(bf16[336,512]{1,0:T(8,128)(2,1)} %copy-done.4) | copy-start | bytes 1032196
  167.0 20.7 %copy-start.9 = (bf16[336,512]{1,0:T(8,128)(2,1)S(1)}, bf16[336,512]{1,0:T(8,128)(2,1)}, u32[]{:S(2)}) copy-start(bf16[336,512]{1,0:T(8,128)(2,1)} %copy-done.8) | copy-start | bytes 1032196
  167.4 60.3 %copy-start.13 = (bf16[336,512]{1,0:T(8,128)(2,1)S(1)}, bf16[336,512]{1,0:T(8,128)(2,1)}, u32[]{:S(2)}) copy-start(bf16[336,512]{1,0:T(8,128)(2,1)} %copy-done.12) | copy-start | bytes 1032196
  167.4 119.5 %copy-start = (bf16[256,5376]{1,0:T(8,128)(2,1)S(1)}, bf16[256,5376]{1,0:T(8,128)(2,1)}, u32[]{:S(2)}) copy-start(bf16[256,5376]{1,0:T(8,128)(2,1)} %param.7) | copy-start | bytes 8257540
  187.6 21.2 %collective-permute-start.10 = (bf16[336,512]{1,0:T(8,128)(2,1)}, bf16[336,512]{1,0:T(8,128)(2,1)S(1)}, u32[]{:S(2)}, u32[]{:S(2)}) collective-permute-start(bf16[336,512]{1,0:T(8,128)(2,1)} %collective-permute-done.9), channel_id=1, source_target_pairs={{0,2},{2,4},{4,6},{6,8},{8,10},{10,12},{12,14},{14,16},{16,18},{18... | collective-permute-start | bytes 1032200 | tf_op jit(solution)/shard_map/ppermute | solution.py:24
  187.7 99.2 %copy-start.14 = (f32[5376]{0:T(1024)}, f32[5376]{0:T(1024)S(1)}, u32[]{:S(2)}) copy-start(f32[5376]{0:T(1024)S(1)} %convert_reduce_fusion) | copy-start | bytes 64516
  208.8 16.8 %collective-permute-start.11 = (bf16[336,512]{1,0:T(8,128)(2,1)S(1)}, bf16[336,512]{1,0:T(8,128)(2,1)S(1)}, u32[]{:S(2)}, u32[]{:S(2)}) collective-permute-start(bf16[336,512]{1,0:T(8,128)(2,1)S(1)} %collective-permute-done.10), channel_id=1, source_target_pairs={{0,2},{2,4},{4,6},{6,8},{8,10},{10,12},{12,14},{14,16},{16,18},{18... | collective-permute-start | bytes 1032200 | tf_op jit(solution)/shard_map/ppermute | solution.py:24
  225.6 21.7 %collective-permute-start.12 = (bf16[336,512]{1,0:T(8,128)(2,1)S(1)}, bf16[336,512]{1,0:T(8,128)(2,1)S(1)}, u32[]{:S(2)}, u32[]{:S(2)}) collective-permute-start(bf16[336,512]{1,0:T(8,128)(2,1)S(1)} %collective-permute-done.11), channel_id=1, source_target_pairs={{0,2},{2,4},{4,6},{6,8},{8,10},{10,12},{12,14},{14,16},{16,18},{18... | collective-permute-start | bytes 1032200 | tf_op jit(solution)/shard_map/ppermute | solution.py:24
  247.3 21.4 %collective-permute-start.13 = (bf16[336,512]{1,0:T(8,128)(2,1)S(1)}, bf16[336,512]{1,0:T(8,128)(2,1)S(1)}, u32[]{:S(2)}, u32[]{:S(2)}) collective-permute-start(bf16[336,512]{1,0:T(8,128)(2,1)S(1)} %collective-permute-done.12), channel_id=1, source_target_pairs={{0,2},{2,4},{4,6},{6,8},{8,10},{10,12},{12,14},{14,16},{16,18},{18... | collective-permute-start | bytes 1032200 | tf_op jit(solution)/shard_map/ppermute | solution.py:24
  268.7 18.1 %collective-permute-start.14 = (bf16[336,512]{1,0:T(8,128)(2,1)S(1)}, bf16[336,512]{1,0:T(8,128)(2,1)S(1)}, u32[]{:S(2)}, u32[]{:S(2)}) collective-permute-start(bf16[336,512]{1,0:T(8,128)(2,1)S(1)} %collective-permute-done.13), channel_id=1, source_target_pairs={{0,2},{2,4},{4,6},{6,8},{8,10},{10,12},{12,14},{14,16},{16,18},{18... | collective-permute-start | bytes 1032200 | tf_op jit(solution)/shard_map/ppermute | solution.py:24
  296.6 10.8 %collective-permute-start.15 = (bf16[256,1024]{1,0:T(8,128)(2,1)S(1)}, bf16[256,1024]{1,0:T(8,128)(2,1)S(1)}, u32[]{:S(2)}, u32[]{:S(2)}) collective-permute-start(bf16[256,1024]{1,0:T(8,128)(2,1)S(1)} %pad_maximum_fusion), channel_id=1, source_target_pairs={{0,2},{2,4},{4,6},{6,8},{8,10},{10,12},{12,14},{14,16},{16,18},{18... | collective-permute-start | bytes 1572872 | tf_op jit(solution)/shard_map/ppermute | solution.py:31
  307.4 14.7 %collective-permute-start.16 = (bf16[256,1024]{1,0:T(8,128)(2,1)S(1)}, bf16[256,1024]{1,0:T(8,128)(2,1)S(1)}, u32[]{:S(2)}, u32[]{:S(2)}) collective-permute-start(bf16[256,1024]{1,0:T(8,128)(2,1)S(1)} %collective-permute-done.15), channel_id=1, source_target_pairs={{0,2},{2,4},{4,6},{6,8},{8,10},{10,12},{12,14},{14,16},{16,18},{18... | collective-permute-start | bytes 1572872 | tf_op jit(solution)/shard_map/ppermute | solution.py:31
  322.1 12.5 %collective-permute-start.17 = (bf16[256,1024]{1,0:T(8,128)(2,1)S(1)}, bf16[256,1024]{1,0:T(8,128)(2,1)}, u32[]{:S(2)}, u32[]{:S(2)}) collective-permute-start(bf16[256,1024]{1,0:T(8,128)(2,1)S(1)} %collective-permute-done.16), channel_id=1, source_target_pairs={{0,2},{2,4},{4,6},{6,8},{8,10},{10,12},{12,14},{14,16},{16,18},{18... | collective-permute-start | bytes 1572872 | tf_op jit(solution)/shard_map/ppermute | solution.py:31
  334.6 11.5 %collective-permute-start.18 = (bf16[256,1024]{1,0:T(8,128)(2,1)}, bf16[256,1024]{1,0:T(8,128)(2,1)S(1)}, u32[]{:S(2)}, u32[]{:S(2)}) collective-permute-start(bf16[256,1024]{1,0:T(8,128)(2,1)} %collective-permute-done.17), channel_id=1, source_target_pairs={{0,2},{2,4},{4,6},{6,8},{8,10},{10,12},{12,14},{14,16},{16,18},{18... | collective-permute-start | bytes 1572872 | tf_op jit(solution)/shard_map/ppermute | solution.py:31
  347.4 6.2 %copy-start.15 = (f32[5376]{0:T(1024)S(1)}, f32[5376]{0:T(1024)}, u32[]{:S(2)}) copy-start(f32[5376]{0:T(1024)} %copy-done.14) | copy-start | bytes 64516
  361.7 1.3 copy-start.1
  363.0 2.6 copy-start.2
  487.1 2.9 copy-start.17
Sparse Core Ops, SparseCore 0:
  10.2 113.6 all-gather.6
  126.6 177.7 all-gather.8
  307.2 168.2 all-gather.10
  490.1 8.5 reduce-scatter.3
